TPU v7x, 128 devices: a whole 4x4x4 slice. The times are simulated.
128 devices in a mesh: feat: 4 (over x), node: 32 (over z, y, core).
Axes of the slice: x: 4, y: 4, z: 4, core: 2. Of those that a mesh axis runs over, the one named last changes fastest.
Arguments:
- features: bfloat16 [65536, 2048], P('node', 'feat'), may hold values from -6 to 6
- self_w1: bfloat16 [2048, 1024], P('feat'), may hold values from -0.125 to 0.125
- neigh_w1: bfloat16 [2048, 1024], P('feat'), may hold values from -0.125 to 0.125
- self_w2: bfloat16 [1024, 1024], P('feat'), may hold values from -0.1875 to 0.1875
- neigh_w2: bfloat16 [1024, 1024], P('feat'), may hold values from -0.1875 to 0.1875
- source_tiles1: int32 [1024], P('node'), may hold values from 0 to 15
- owner_blocks1: int32 [1024, 1], P('node'), may hold values from 0 to 31; in each aligned block of 32 rows (0 to 31, 32 to 63, ...) at most 2 rows name the same one
- target_tiles1: int32 [1024], P('node'), may hold values from 0 to 15
- tile_masks1: int32 [1024, 128, 128], P('node'), may hold values 0 or 1
- source_tiles2: int32 [1024], P('node'), may hold values from 0 to 15
- owner_blocks2: int32 [1024, 1], P('node'), may hold values from 0 to 31; in each aligned block of 32 rows (0 to 31, 32 to 63, ...) at most 2 rows name the same one
- target_tiles2: int32 [1024], P('node'), may hold values from 0 to 15
- tile_masks2: int32 [1024, 128, 128], P('node'), may hold values 0 or 1
- cotangent: bfloat16 [65536, 1024], P('node', 'feat'), may hold values from -0.0234375 to 0.0234375
Outputs:
- hidden2: bfloat16 [65536, 1024], P('node', 'feat')
- grad_self2: float32 [1024, 1024], P(('feat', 'node'))
- grad_neigh2: float32 [1024, 1024], P(('feat', 'node'))
Inputs may be any that keep to these rules, and one draw needn't show every extreme that they name: `owner_blocks1`: among the 32 entries of one node block, at most 2 name the same written block. `owner_blocks2`: among the 32 entries of one node block, at most 2 name the same written block.
All inputs are finite; a program needn't handle non-finite values. No bound on the sum of `tile_masks1` or of `tile_masks2` on one device may be relied on, other than what follows from the above.
Results may differ from a plain program's by a relative error of at most 0.0061.
Values may be sent and summed in bfloat16 or wider, within the bound.
A program may use at most 128 MiB of HBM per device.

v0:
```python
import jax
import jax.numpy as jnp
from jax import lax
from jax.sharding import PartitionSpec as P


def pack_tiles(values, source_tiles, owner_blocks, target_tiles, tile_masks, owners):
    tile_size = tile_masks.shape[1]
    entries = tile_masks.shape[0]
    feature_width = values.shape[1]
    tiles_here = values.shape[0] // tile_size
    capacity = max(2, 4 * tiles_here // owners)
    blocks = values.reshape(tiles_here, tile_size, feature_width)
    picked = jnp.take(blocks, source_tiles, axis=0)
    masks_bf = tile_masks.astype(jnp.bfloat16)
    pieces = jnp.einsum(
        "eac,eaw->ecw", masks_bf, picked, preferred_element_type=jnp.float32
    ).astype(jnp.bfloat16)
    counts = jnp.sum(tile_masks, axis=1).astype(jnp.bfloat16)
    owner_ids = owner_blocks[:, 0]
    owner_hot = (owner_ids[:, None] == jnp.arange(owners, dtype=jnp.int32)[None, :]).astype(
        jnp.int32
    )
    slot_rank = jnp.sum((jnp.cumsum(owner_hot, axis=0) - owner_hot) * owner_hot, axis=1)
    slot_index = owner_ids * capacity + slot_rank
    slot_hot = (
        jnp.arange(owners * capacity, dtype=jnp.int32)[:, None] == slot_index[None, :]
    ).astype(jnp.bfloat16)
    flat_pieces = pieces.reshape(entries, tile_size * feature_width)
    sent_pieces = jnp.dot(slot_hot, flat_pieces, preferred_element_type=jnp.float32).astype(
        jnp.bfloat16
    )
    sent_pieces = sent_pieces.reshape(owners * capacity, tile_size, feature_width)
    sent_counts = jnp.dot(slot_hot, counts, preferred_element_type=jnp.float32).astype(jnp.bfloat16)
    target_hot = (target_tiles[:, None] == jnp.arange(tiles_here, dtype=jnp.int32)[None, :]).astype(
        jnp.bfloat16
    )
    sent_targets = jnp.dot(slot_hot, target_hot, preferred_element_type=jnp.float32).astype(
        jnp.bfloat16
    )
    return (sent_pieces, sent_counts, sent_targets)


def unpack_tiles(got_pieces, got_counts, got_targets):
    slots, tile_size, feature_width = got_pieces.shape
    tiles_here = got_targets.shape[1]
    flat_pieces = got_pieces.reshape(slots, tile_size * feature_width)
    summed = jnp.einsum("st,sx->tx", got_targets, flat_pieces, preferred_element_type=jnp.float32)
    degree = jnp.einsum("st,sc->tc", got_targets, got_counts, preferred_element_type=jnp.float32)
    summed = summed.reshape(tiles_here, tile_size, feature_width)
    mean_rows = summed / jnp.maximum(degree, 1.0)[:, :, None]
    return mean_rows.reshape(tiles_here * tile_size, feature_width)


def local(
    features,
    self_w1,
    neigh_w1,
    self_w2,
    neigh_w2,
    source_tiles1,
    owner_blocks1,
    target_tiles1,
    tile_masks1,
    source_tiles2,
    owner_blocks2,
    target_tiles2,
    tile_masks2,
    cotangent,
):
    owners = lax.axis_size("node")
    self_term = jnp.dot(features, self_w1, preferred_element_type=jnp.float32)
    neigh_term = jnp.dot(features, neigh_w1, preferred_element_type=jnp.float32)
    self1, neigh_sum = (
        lax.psum_scatter(self_term, "feat", scatter_dimension=1, tiled=True),
        lax.psum_scatter(neigh_term, "feat", scatter_dimension=1, tiled=True),
    )
    proj1 = neigh_sum.astype(jnp.bfloat16)
    packed1 = pack_tiles(proj1, source_tiles1, owner_blocks1, target_tiles1, tile_masks1, owners)
    got_pieces1, got_counts1, got_targets1 = (
        lax.all_to_all(packed1[0], "node", split_axis=0, concat_axis=0, tiled=True),
        lax.all_to_all(packed1[1], "node", split_axis=0, concat_axis=0, tiled=True),
        lax.all_to_all(packed1[2], "node", split_axis=0, concat_axis=0, tiled=True),
    )
    mean1 = unpack_tiles(got_pieces1, got_counts1, got_targets1)
    hidden1 = jax.nn.relu(self1 + mean1).astype(jnp.bfloat16)
    packed2 = pack_tiles(hidden1, source_tiles2, owner_blocks2, target_tiles2, tile_masks2, owners)
    got_pieces2, got_counts2, got_targets2 = (
        lax.all_to_all(packed2[0], "node", split_axis=0, concat_axis=0, tiled=True),
        lax.all_to_all(packed2[1], "node", split_axis=0, concat_axis=0, tiled=True),
        lax.all_to_all(packed2[2], "node", split_axis=0, concat_axis=0, tiled=True),
    )
    mean2 = unpack_tiles(got_pieces2, got_counts2, got_targets2).astype(jnp.bfloat16)
    layer_term = jnp.dot(hidden1, self_w2, preferred_element_type=jnp.float32) + jnp.dot(
        mean2, neigh_w2, preferred_element_type=jnp.float32
    )
    pre2 = lax.psum_scatter(layer_term, "feat", scatter_dimension=1, tiled=True)
    sigma = jax.nn.sigmoid(pre2)
    hidden2 = (pre2 * sigma).astype(jnp.bfloat16)
    slope = (cotangent.astype(jnp.float32) * sigma * (1.0 + pre2 * (1.0 - sigma))).astype(
        jnp.bfloat16
    )
    slope_full = lax.all_gather(slope, "feat", axis=1, tiled=True)
    contract_rows = (((0,), (0,)), ((), ()))
    grads = lax.psum_scatter(
        jnp.concatenate(
            [
                lax.dot_general(
                    hidden1, slope_full, contract_rows, preferred_element_type=jnp.float32
                ),
                lax.dot_general(
                    mean2, slope_full, contract_rows, preferred_element_type=jnp.float32
                ),
            ],
            axis=1,
        ),
        "node",
        scatter_dimension=0,
        tiled=True,
    )
    full_width = slope_full.shape[1]
    return (hidden2, grads[:, :full_width], grads[:, full_width:])


def solution(mesh):
    in_specs = (
        P("node", "feat"),
        P("feat", None),
        P("feat", None),
        P("feat", None),
        P("feat", None),
        P("node"),
        P("node", None),
        P("node"),
        P("node", None, None),
        P("node"),
        P("node", None),
        P("node"),
        P("node", None, None),
        P("node", "feat"),
    )
    out_specs = (P("node", "feat"), P(("feat", "node"), None), P(("feat", "node"), None))
    return jax.shard_map(local, mesh=mesh, in_specs=in_specs, out_specs=out_specs, check_vma=False)
```

profile of v0, /device:TPU:1, one launch (start us, length us, event | category | flops | bytes accessed | tf_op | source)
XLA Modules:
  0.0 518.1 jit_solution(2008605957858048572)
XLA Ops:
  8.8 6.8 %fusion.49 = f32[2048,1024]{1,0:T(8,128)} fusion(bf16[2048,512]{1,0:T(8,128)(2,1)S(1)} %copy-done, bf16[512,1024]{1,0:T(8,128)(2,1)} %param.18), kind=kOutput, calls=%fused_computation.78 | convolution fusion | flops 2147483648 | bytes 11534336 | tf_op jit(solution)/shard_map/dot_general | solution.py:73
  16.8 5.6 %fusion.48 = f32[2048,1024]{1,0:T(8,128)} fusion(bf16[2048,512]{1,0:T(8,128)(2,1)S(1)} %copy-done, bf16[512,1024]{1,0:T(8,128)(2,1)S(1)} %copy-done.11), kind=kOutput, calls=%fused_computation.77 | convolution fusion | flops 2147483648 | bytes 11534336 | tf_op jit(solution)/shard_map/dot_general | solution.py:72
  24.3 9.6 %all-to-all-start = ((bf16[32,2,16]{2,1,0:T(2,128)(2,1)}), bf16[32,2,16]{2,1,0:T(2,128)(2,1)S(1)}, u32[]{:S(2)}, u32[]{:S(2)}) async-start(bf16[32,2,16]{2,1,0:T(2,128)(2,1)} %bitcast.1), calls=%async_computation.1 | async-start | bytes 32768 | tf_op jit(solution)/shard_map/all_to_all | solution.py:83
  34.8 64.7 %reduce-scatter.7.cloned.1.call-done = f32[2048,256]{1,0:T(8,128)} async-done(((f32[2048,1024]{1,0:T(8,128)}), f32[2048,256]{1,0:T(8,128)}) %reduce-scatter.7.cloned.1.call-update) | async-done | bytes 2097168 | tf_op jit(solution)/shard_map/reduce_scatter | solution.py:76
  101.2 2.1 gather_fusion
  103.2 4.5 convert_bitcast_fusion.1
  107.7 3.4 copy.72
  111.1 7.7 %all-to-all-start.2 = ((bf16[32,2,128]{2,1,0:T(2,128)(2,1)}), bf16[32,2,128]{2,1,0:T(2,128)(2,1)S(1)}, u32[]{:S(2)}, u32[]{:S(2)}) async-start(bf16[32,2,128]{2,1,0:T(2,128)(2,1)} %bitcast.7), calls=%async_computation.4 | async-start | bytes 32768 | tf_op jit(solution)/shard_map/all_to_all | solution.py:82
  120.0 3.0 copy.73
  123.0 2.6 all-to-all-done.2
  125.7 5.2 %all-to-all-start.1 = ((bf16[64,128,256]{2,1,0:T(8,128)(2,1)}), bf16[64,128,256]{2,1,0:T(8,128)(2,1)}, u32[]{:S(2)}, u32[]{:S(2)}) async-start(bf16[64,128,256]{2,1,0:T(8,128)(2,1)} %bitcast.88), calls=%async_computation.3 | async-start | bytes 8388608 | tf_op jit(solution)/shard_map/all_to_all | solution.py:81
  133.4 47.9 %all-to-all-done.1 = bf16[64,128,256]{2,1,0:T(8,128)(2,1)} async-done(((bf16[64,128,256]{2,1,0:T(8,128)(2,1)}), bf16[64,128,256]{2,1,0:T(8,128)(2,1)}, u32[]{:S(2)}, u32[]{:S(2)}) %all-to-all-start.1) | async-done | bytes 4194336 | tf_op jit(solution)/shard_map/all_to_all | solution.py:81
  181.3 7.0 %all-to-all-start.3 = ((bf16[32,2,16]{2,1,0:T(2,128)(2,1)}), bf16[32,2,16]{2,1,0:T(2,128)(2,1)S(1)}, u32[]{:S(2)}, u32[]{:S(2)}) async-start(bf16[32,2,16]{2,1,0:T(2,128)(2,1)} %bitcast.11), calls=%async_computation.5 | async-start | bytes 32768 | tf_op jit(solution)/shard_map/all_to_all | solution.py:91
  188.3 5.1 fusion.18
  193.4 2.6 copy.54
  196.0 2.5 fusion.7
  198.5 2.0 gather_fusion.1
  200.5 4.5 convert_bitcast_fusion
  205.0 4.5 copy.75
  209.5 7.5 %all-to-all-start.5 = ((bf16[32,2,128]{2,1,0:T(2,128)(2,1)}), bf16[32,2,128]{2,1,0:T(2,128)(2,1)S(1)}, u32[]{:S(2)}, u32[]{:S(2)}) async-start(bf16[32,2,128]{2,1,0:T(2,128)(2,1)} %bitcast.17), calls=%async_computation.7 | async-start | bytes 32768 | tf_op jit(solution)/shard_map/all_to_all | solution.py:90
  217.0 2.8 convolution_convert_fusion
  219.8 3.0 copy.76
  223.9 6.5 %all-to-all-start.4 = ((bf16[64,128,256]{2,1,0:T(8,128)(2,1)}), bf16[64,128,256]{2,1,0:T(8,128)(2,1)}, u32[]{:S(2)}, u32[]{:S(2)}) async-start(bf16[64,128,256]{2,1,0:T(8,128)(2,1)} %bitcast.89), calls=%async_computation.6 | async-start | bytes 8388608 | tf_op jit(solution)/shard_map/all_to_all | solution.py:89
  231.0 4.5 fusion.50
  235.4 45.2 %all-to-all-done.4 = bf16[64,128,256]{2,1,0:T(8,128)(2,1)} async-done(((bf16[64,128,256]{2,1,0:T(8,128)(2,1)}), bf16[64,128,256]{2,1,0:T(8,128)(2,1)}, u32[]{:S(2)}, u32[]{:S(2)}) %all-to-all-start.4) | async-done | bytes 4194336 | tf_op jit(solution)/shard_map/all_to_all | solution.py:89
  280.7 4.7 divide_convert_fusion
  286.4 4.5 convolution_add_fusion
  291.0 78.6 %reduce-scatter.9.cloned.1.call-done = f32[2048,256]{1,0:T(8,128)} async-done(((f32[2048,1024]{1,0:T(8,128)}), f32[2048,256]{1,0:T(8,128)}) %reduce-scatter.9.cloned.1.call-update) | async-done | bytes 2097168 | tf_op jit(solution)/shard_map/reduce_scatter | solution.py:97
  369.6 3.8 multiply_convert_fusion
  373.5 50.9 %all-gather.2.cloned.1.call-done = bf16[2048,1024]{1,0:T(8,128)(2,1)} async-done(((bf16[2048,256]{1,0:T(8,128)(2,1)}), bf16[2048,1024]{1,0:T(8,128)(2,1)}) %all-gather.2.cloned.1.call-update) | async-done | bytes 4194320 | tf_op jit(solution)/shard_map/all_gather | solution.py:103
  424.4 3.6 fusion.52
  430.8 79.3 %reduce-scatter.11.cloned.1.call-done = f32[8,2048]{1,0:T(8,128)} async-done(((f32[256,2048]{1,0:T(8,128)}), f32[8,2048]{1,0:T(8,128)}) %reduce-scatter.11.cloned.1.call-update) | async-done | bytes 65552 | tf_op jit(solution)/shard_map/reduce_scatter | solution.py:105
  (78 shorter events, 17.9 us)
Async XLA Ops:
  7.2 1.6 copy-start
  7.2 92.3 %reduce-scatter.7.cloned.1.call-start = ((), (), s32[]{:S(2)}) async-start(), calls=%async_computation.11 | async-start | bytes 10485760 | tf_op jit(solution)/shard_map/reduce_scatter | solution.py:76
  15.6 1.2 copy-start.11
  15.6 180.4 %reduce-scatter.5.cloned.1.call-start = ((), (), s32[]{:S(2)}) async-start(), calls=%async_computation.10 | async-start | bytes 10485760 | tf_op jit(solution)/shard_map/reduce_scatter | solution.py:75
  22.3 0.7 copy-start.8
  22.3 1.0 copy-start.12
  22.4 11.6 %copy-start.3 = (s32[32,128,128]{2,1,0:T(8,128)S(1)}, s32[32,128,128]{2,1,0:T(8,128)}, u32[]{:S(2)}) copy-start(s32[32,128,128]{2,1,0:T(8,128)} %param.24) | copy-start | bytes 6291460
  22.4 11.7 %copy-start.13 = (s32[32]{0:T(128)S(1)}, s32[32]{0:T(128)}, u32[]{:S(2)}) copy-start(s32[32]{0:T(128)} %param.21) | copy-start | bytes 388
  24.3 86.8 %all-to-all-start = ((bf16[32,2,16]{2,1,0:T(2,128)(2,1)}), bf16[32,2,16]{2,1,0:T(2,128)(2,1)S(1)}, u32[]{:S(2)}, u32[]{:S(2)}) async-start(bf16[32,2,16]{2,1,0:T(2,128)(2,1)} %bitcast.1), calls=%async_computation.1 | async-start | bytes 32768 | tf_op jit(solution)/shard_map/all_to_all | solution.py:83
  111.1 14.5 %all-to-all-start.2 = ((bf16[32,2,128]{2,1,0:T(2,128)(2,1)}), bf16[32,2,128]{2,1,0:T(2,128)(2,1)S(1)}, u32[]{:S(2)}, u32[]{:S(2)}) async-start(bf16[32,2,128]{2,1,0:T(2,128)(2,1)} %bitcast.7), calls=%async_computation.4 | async-start | bytes 32768 | tf_op jit(solution)/shard_map/all_to_all | solution.py:82
  125.7 5.2 %copy-start.9 = (s32[32,1]{0,1:T(1,128)S(1)}, s32[32,1]{0,1:T(1,128)}, u32[]{:S(2)}) copy-start(s32[32,1]{0,1:T(1,128)} %param.26) | copy-start | bytes 388
  125.7 5.6 %copy-start.14 = (s32[32]{0:T(128)S(1)}, s32[32]{0:T(128)}, u32[]{:S(2)}) copy-start(s32[32]{0:T(128)} %param.27) | copy-start | bytes 388
  125.7 6.5 %copy-start.4 = (s32[32,128,128]{2,1,0:T(8,128)S(1)}, s32[32,128,128]{2,1,0:T(8,128)}, u32[]{:S(2)}) copy-start(s32[32,128,128]{2,1,0:T(8,128)} %param.28) | copy-start | bytes 6291460
  125.7 55.6 %all-to-all-start.1 = ((bf16[64,128,256]{2,1,0:T(8,128)(2,1)}), bf16[64,128,256]{2,1,0:T(8,128)(2,1)}, u32[]{:S(2)}, u32[]{:S(2)}) async-start(bf16[64,128,256]{2,1,0:T(8,128)(2,1)} %bitcast.88), calls=%async_computation.3 | async-start | bytes 8388608 | tf_op jit(solution)/shard_map/all_to_all | solution.py:81
  130.9 1.4 copy-start.15
  181.3 28.2 %all-to-all-start.3 = ((bf16[32,2,16]{2,1,0:T(2,128)(2,1)}), bf16[32,2,16]{2,1,0:T(2,128)(2,1)S(1)}, u32[]{:S(2)}, u32[]{:S(2)}) async-start(bf16[32,2,16]{2,1,0:T(2,128)(2,1)} %bitcast.11), calls=%async_computation.5 | async-start | bytes 32768 | tf_op jit(solution)/shard_map/all_to_all | solution.py:91
  209.5 14.4 %all-to-all-start.5 = ((bf16[32,2,128]{2,1,0:T(2,128)(2,1)}), bf16[32,2,128]{2,1,0:T(2,128)(2,1)S(1)}, u32[]{:S(2)}, u32[]{:S(2)}) async-start(bf16[32,2,128]{2,1,0:T(2,128)(2,1)} %bitcast.17), calls=%async_computation.7 | async-start | bytes 32768 | tf_op jit(solution)/shard_map/all_to_all | solution.py:90
  223.9 7.1 %copy-start.7 = (bf16[256,1024]{1,0:T(8,128)(2,1)S(1)}, bf16[256,1024]{1,0:T(8,128)(2,1)}, u32[]{:S(2)}) copy-start(bf16[256,1024]{1,0:T(8,128)(2,1)} %param.19) | copy-start | bytes 1572868
  223.9 56.8 %all-to-all-start.4 = ((bf16[64,128,256]{2,1,0:T(8,128)(2,1)}), bf16[64,128,256]{2,1,0:T(8,128)(2,1)}, u32[]{:S(2)}, u32[]{:S(2)}) async-start(bf16[64,128,256]{2,1,0:T(8,128)(2,1)} %bitcast.89), calls=%async_computation.6 | async-start | bytes 8388608 | tf_op jit(solution)/shard_map/all_to_all | solution.py:89
  230.4 139.2 %reduce-scatter.9.cloned.1.call-start = ((), (), s32[]{:S(2)}) async-start(), calls=%async_computation.12 | async-start | bytes 10485760 | tf_op jit(solution)/shard_map/reduce_scatter | solution.py:97
  280.7 5.1 copy-start.2
  285.4 1.0 copy-start.6
  290.9 78.7 %copy-start.5 = (bf16[2048,256]{1,0:T(8,128)(2,1)S(1)}, bf16[2048,256]{1,0:T(8,128)(2,1)}, u32[]{:S(2)}) copy-start(bf16[2048,256]{1,0:T(8,128)(2,1)} %param.29) | copy-start | bytes 3145732
  290.9 133.5 %all-gather.2.cloned.1.call-start = ((), (), s32[]{:S(2)}) async-start(), calls=%async_computation.13 | async-start | bytes 5242880 | tf_op jit(solution)/shard_map/all_gather | solution.py:103
  373.4 136.7 %reduce-scatter.11.cloned.1.call-start = ((), (), s32[]{:S(2)}) async-start(), calls=%async_computation.14 | async-start | bytes 2162688 | tf_op jit(solution)/shard_map/reduce_scatter | solution.py:105
  424.4 3.6 copy-start.10
  429.3 82.2 %copy-start.1 = (bf16[2048,512]{1,0:T(8,128)(2,1)S(1)}, bf16[2048,512]{1,0:T(8,128)(2,1)}, u32[]{:S(2)}) copy-start(bf16[2048,512]{1,0:T(8,128)(2,1)} %param.16) | copy-start | bytes 6291460
Sparse Core Ops, SparseCore 0:
  15.7 83.7 reduce-scatter.6
  102.0 80.2 reduce-scatter.4
  291.0 78.5 reduce-scatter.8
  373.6 50.7 all-gather.1
  431.0 79.1 reduce-scatter.10
where the time goes:
time: 520 us; the launch traced here: 518 us
  waiting for transfers between devices  370 us (71%)
  matrix products  51.3 us (10%)
  starting transfers between devices  44 us (8%)
  local copies, waits for them, and re-layouts  28 us (5%)
  between operations  14.1 us (3%)
  other arithmetic  10.4 us (2%)
    reduce_scatter x1, waiting for transfers between devices, local(): lax.psum_scatter(jnp.concatenate([lax.dot_general(hidden1, slope_full, co...  79.3 us
    reduce_scatter x1, waiting for transfers between devices, local(): pre2 = lax.psum_scatter(layer_term, 'feat', scatter_dimension=1, tiled=True)  78.6 us
    reduce_scatter x1, waiting for transfers between devices, local(): lax.psum_scatter(neigh_term, 'feat', scatter_dimension=1, tiled=True)  64.7 us
    all_gather x1, waiting for transfers between devices, local(): slope_full = lax.all_gather(slope, 'feat', axis=1, tiled=True)  50.9 us
    all_to_all x1, waiting for transfers between devices, local(): lax.all_to_all(packed1[0], 'node', split_axis=0, concat_axis=0, tiled=True)  47.9 us
    all_to_all x1, waiting for transfers between devices, local(): lax.all_to_all(packed2[0], 'node', split_axis=0, concat_axis=0, tiled=True)  45.2 us
    unnamed x36, local copies, waits for them, and re-layouts  18 us
  transfers between devices with their start and end apart: 11, of which 8 were waited for; matrix products, arithmetic and copies ran while one was open for 11% of the time, Pallas kernels for 0%

commit v1 on v0

v1 whole, which is shorter than its diff:
```python
import functools

import jax
import jax.numpy as jnp
from jax import lax
from jax.experimental import pallas as pl
from jax.experimental.pallas import tpu as pltpu
from jax.sharding import PartitionSpec as P

MESH = pl.DeviceIdType.MESH
BF = jnp.bfloat16
F32 = jnp.float32
NEIGH, SELF = 0, 1


def dot(a, b):
    return jnp.dot(a, b, preferred_element_type=F32)


def kernel(
    feat_hbm, ws1_hbm, wn1_hbm, ws2_hbm, wn2_hbm,
    src1, own1, tgt1, mask1_hbm, src2, own2, tgt2, mask2_hbm, cot_hbm,
    hid2_out, gs_out, gn_out,
    feat, w1n, w1s, mask1, mask2, maskt, cnt, tab,
    p0, p1, p2, p3, own, a0, a1, a2, a3, b0, b1, b2, b3, proj0, proj1, hid0, hid1,
    msg_out, msg_in, vcol, ccol, lhs, rdeg,
    send0, send1, recv0, recv1, recv2, recv3, h0, h1, m0, m1, xoth0, xoth1, xt,
    cot, w2, slope_own, slope_oth,
    g0, g1, r1a, r1b, s1a, s1b, r2a, r2b, s2a, s2b, r3a, r3b, fin, finr,
    ld, meta_s, meta_r, ra_s, ra_r, rb_s, rb_r, aa_s, aa_r, rows_s, rows_r,
    cot_s, cot_r, w2_s, w2_r, wd_s, wd_r, x_s, x_r, sl_s, sl_r, h2_s, h2_r,
    g1_s, g1_r, g2_s, g2_r, g3_s, g3_r, fn_s, fn_r,
):
    f = lax.axis_index("feat")
    n = lax.axis_index("node")
    z, y, core = n // 8, (n // 2) % 4, n % 2
    sign = 1 - 2 * core
    right, left, opp = (f + 1) % 4, (f + 3) % 4, (f + 2) % 4
    other = n + sign
    proj, hid = (proj0, proj1), (hid0, hid1)
    psend, buf_a, buf_b = (p0, p1, p2, p3), (a0, a1, a2, a3), (b0, b1, b2, b3)
    sendbuf, recv = (send0, send1), (recv0, recv1, recv2, recv3)
    hm, xoth = ((h0, h1), (m0, m1)), (xoth0, xoth1)
    r1, s1, r2, s2, r3 = (r1a, r1b), (s1a, s1b), (r2a, r2b), (s2a, s2b), (r3a, r3b)

    def peer(i):
        j, ii, dc = i // 8, (i // 2) % 4, i % 2
        zz = (z + sign * ii + 4) % 4
        yy = (y + sign * ((ii + j) % 4) + 4) % 4
        return (f, zz * 8 + yy * 2 + (core + dc) % 2)

    def remote(src, dst, ss, rs, dev):
        return pltpu.make_async_remote_copy(
            src_ref=src, dst_ref=dst, send_sem=ss, recv_sem=rs, device_id=dev, device_id_type=MESH
        )

    def local(src, dst, k):
        return pltpu.make_async_copy(src, dst, ld.at[k])

    loads = [
        local(feat_hbm, feat, 0),
        local(wn1_hbm, w1n, 1),
        local(ws1_hbm, w1s, 2),
        local(mask1_hbm, mask1, 3),
        local(cot_hbm.at[pl.ds(pl.multiple_of(f * 512, 512), 512)], cot.at[f], 4),
    ]
    for m, ref in ((0, ws2_hbm), (1, wn2_hbm)):
        for c in range(2):
            loads.append(local(ref.at[pl.ds(c * 128, 128)], w2.at[m, f, c], 5 + 2 * m + c))
    load_mask2 = local(mask2_hbm, mask2, 9)
    for c in [*loads, load_mask2]:
        c.start()

    barrier = pltpu.get_barrier_semaphore()

    @pl.loop(1, 32)
    def _(i):
        pl.semaphore_signal(barrier, inc=1, device_id=peer(i), device_id_type=MESH)

    for d in (right, left, opp):
        pl.semaphore_signal(barrier, inc=1, device_id=(d, n), device_id_type=MESH)
    pl.semaphore_wait(barrier, 34)

    def project(mat, j, where):
        cols = pl.ds(pl.multiple_of(j * 256, 256), 256)

        @pl.loop(0, 4)
        def _(t):
            rows = pl.ds(pl.multiple_of(t * 512, 512), 512)
            part = dot(feat[rows, :], (w1n, w1s)[mat][:, cols])
            for c in range(2):
                half = part[:, c * 128 : (c + 1) * 128]
                if where is None:
                    own[2 * mat + c, pl.ds(t * 4, 4)] = half.reshape(4, 128, 128)
                else:
                    psend[2 * mat + c][where, rows, :] = half.astype(BF)

    lo, hi = pl.ds(0, 1024), pl.ds(1024, 1024)

    def copies_a(q):
        return [
            remote(psend[q].at[0, lo], buf_a[q].at[0], ra_s.at[q, 0], ra_r.at[q, 0], (right, n)),
            remote(psend[q].at[0, hi], buf_a[q].at[1], ra_s.at[q, 1], ra_r.at[q, 1], (left, n)),
        ]

    def copies_direct(q):
        return [
            remote(psend[q].at[1, hi], buf_b[q].at[0, hi], rb_s.at[q, 0], rb_r.at[q, 0], (right, n)),
            remote(psend[q].at[2, lo], buf_b[q].at[1, lo], rb_s.at[q, 1], rb_r.at[q, 1], (left, n)),
        ]

    def copies_added(q):
        return [
            remote(psend[q].at[1, lo], buf_b[q].at[0, lo], rb_s.at[q, 2], rb_r.at[q, 2], (right, n)),
            remote(psend[q].at[2, hi], buf_b[q].at[1, hi], rb_s.at[q, 3], rb_r.at[q, 3], (left, n)),
        ]

    def start(copies):
        for c in copies:
            c.start()

    def ring_start(q):
        start(copies_a(q))
        start(copies_direct(q))

    def ring_add(q):
        a, b = copies_a(q), copies_added(q)
        for s, base in ((0, 0), (1, 1024)):
            a[s].wait_recv()

            @pl.loop(0, 4)
            def _(t):
                rows = pl.ds(pl.multiple_of(t * 256 + base, 256), 256)
                from_rows = pl.ds(pl.multiple_of(t * 256, 256), 256)
                total = psend[q][1 + s, rows, :].astype(F32) + buf_a[q][s, from_rows, :].astype(F32)
                psend[q][1 + s, rows, :] = total.astype(BF)

            b[s].start()

    def ring_end(q):
        for c in copies_direct(q) + copies_added(q):
            c.wait_recv()

        @pl.loop(0, 8)
        def _(t):
            rows = pl.ds(pl.multiple_of(t * 256, 256), 256)
            got = buf_b[q][0, rows, :].astype(F32) + buf_b[q][1, rows, :].astype(F32)
            total = own[q, pl.ds(t * 2, 2)] + got.reshape(2, 128, 128)
            if q < 2:
                proj[q][pl.ds(t * 2, 2)] = total.astype(BF)
            else:
                own[q, pl.ds(t * 2, 2)] = total

    def masks_of(layer, mask):
        @pl.loop(0, 32)
        def _(e):
            m = mask[e].astype(F32)
            cnt[layer, e] = jnp.broadcast_to(jnp.sum(m, axis=0, keepdims=True), (8, 128))
            maskt[layer, e] = m.T.astype(BF)

    def slots_of(layer, owners, sources):
        @pl.loop(0, 32)
        def _(i):
            who = peer(i)[1]

            def look(e, carry):
                seen, first, second = carry
                hit = owners[e, 0] == who
                first = jnp.where(jnp.logical_and(hit, seen == 0), e, first)
                second = jnp.where(jnp.logical_and(hit, seen == 1), e, second)
                return seen + hit.astype(jnp.int32), first, second

            zero = jnp.int32(0)
            seen, first, second = lax.fori_loop(0, 32, look, (zero, zero, zero), unroll=8)
            tab[layer, i, 0] = first
            tab[layer, i, 1] = second
            tab[layer, i, 2] = sources[first]
            tab[layer, i, 3] = sources[second]
            tab[layer, i, 4] = seen

    def meta_copy(i):
        return remote(msg_out.at[i], msg_in.at[i], meta_s.at[i], meta_r.at[i], peer(i))

    def message(i):
        row = lax.broadcasted_iota(jnp.int32, (8, 128), 0)
        msg = jnp.zeros((8, 128), F32)
        for layer, targets in ((0, tgt1), (1, tgt2)):
            for k in range(2):
                e = tab[layer, i, k]
                used = tab[layer, i, 4] > k
                place = jnp.where(used, targets[e] * 16, -1024).astype(F32)
                msg = jnp.where(row == layer * 4 + k, cnt[layer, e], msg)
                msg = jnp.where(row == layer * 4 + 2 + k, place, msg)
        return msg

    def meta_send():
        msg_in[0] = message(0)

        @pl.loop(1, 32)
        def _(i):
            msg_out[i] = message(i)
            meta_copy(i).start()

    def meta_wait():
        @pl.loop(1, 32)
        def _(i):
            meta_copy(i).wait()

    def build(layer):
        @pl.loop(0, 32)
        def _(i):
            msg = msg_in[i]
            for k in range(2):
                rows = pl.ds(pl.multiple_of(i * 32 + k * 16, 16), 16)
                place = msg[layer * 4 + 2 + k : layer * 4 + 3 + k, :]
                vcol[rows, :] = jnp.broadcast_to(place, (16, 128))
                count = msg[layer * 4 + k : layer * 4 + k + 1, :]
                ccol[rows, :] = jnp.broadcast_to(count, (16, 128)).astype(BF)

        ramp = lax.broadcasted_iota(jnp.int32, (1024, 128), 0) % 16
        vrow = (vcol[...] + ramp.astype(F32)).T[0:1, :]
        spot = lax.broadcasted_iota(jnp.int32, (256, 1024), 0).astype(F32)
        lhs[layer] = jnp.where(spot == vrow, 1.0, 0.0).astype(BF)
        degree = dot(lhs[layer], ccol[...])
        lane = lax.broadcasted_iota(jnp.int32, (256, 128), 1)
        within = lax.broadcasted_iota(jnp.int32, (256, 128), 0) % 16
        for g in range(8):
            here = jnp.sum(jnp.where(lane == within + g * 16, degree, 0.0), axis=1, keepdims=True)
            rdeg[g] = jnp.broadcast_to(1.0 / jnp.maximum(here, 1.0), (256, 128))

    def piece_copy(phase, i):
        c = phase % 2
        return remote(
            sendbuf[c].at[i], recv[phase].at[i], aa_s.at[phase, i], aa_r.at[phase, i], peer(i)
        )

    def piece(layer, values, c, i, k):
        return dot(maskt[layer, tab[layer, i, k]], values[c][tab[layer, i, 2 + k]]).astype(BF)

    def pieces(phase, values):
        layer, c = phase // 2, phase % 2
        if layer == 1:

            @pl.loop(1, 32)
            def _(i):
                piece_copy(c, i).wait_send()

        @pl.loop(1, 32)
        def _(i):
            for k in range(2):
                sendbuf[c][i, k] = piece(layer, values, c, i, k)
            piece_copy(phase, i).start()

        for k in range(2):
            recv[phase][0, k] = piece(layer, values, c, 0, k)

    def gather_tiles(phase, result):
        layer, c = phase // 2, phase % 2

        @pl.loop(1, 32)
        def _(i):
            piece_copy(phase, i).wait_recv()

        for g in range(8):
            rows = pl.ds(g * 16, 16)
            got = recv[phase][:, :, rows, :].reshape(1024, 128)
            mean = dot(lhs[layer], got) * rdeg[g]
            if layer == 0:
                mean = jnp.maximum(own[2 + c, :, rows, :].reshape(256, 128) + mean, 0.0)
            result[c][:, rows, :] = mean.astype(BF).reshape(16, 16, 128)

    far = (right, left, opp)
    back = (1, 0, 2)

    def rows_copies(m, c, values):
        return [
            remote(
                values[c].at[pl.ds(d * 4, 4)], hm[m][c].at[f],
                rows_s.at[m, c, k], rows_r.at[m, c, k], (d, n),
            )
            for k, d in enumerate(far)
        ]

    def rows_send(m, c, values):
        start(rows_copies(m, c, values))
        hm[m][c][f] = values[c][pl.ds(f * 4, 4)]

    def rows_wait(m, c, values):
        for copy in rows_copies(m, c, values):
            copy.wait_recv()

    def cot_copies():
        return [
            remote(
                cot_hbm.at[pl.ds(pl.multiple_of(d * 512, 512), 512)], cot.at[f],
                cot_s.at[k], cot_r.at[k], (d, n),
            )
            for k, d in enumerate(far)
        ]

    def w2_copies(d, k):
        return remote(
            w2.at[core, f], w2.at[core, f], w2_s.at[k], w2_r.at[k], (d, n)
        )

    def w2_forward(d, k):
        return remote(
            w2.at[core, d], w2.at[core, d], wd_s.at[k], wd_r.at[k], (f, other)
        )

    def pre_add(m, c, first):
        left_side = jnp.concatenate([hm[m][c][s].reshape(512, 128) for s in range(4)], axis=1)

        @pl.loop(0, 4)
        def _(j):
            cols = pl.ds(pl.multiple_of(j * 256, 256), 256)
            part = dot(left_side, w2[m, :, c, :, cols].reshape(512, 256))
            for half in range(2):
                new = part[:, half * 128 : (half + 1) * 128].reshape(4, 128, 128)
                at = pl.ds(j * 4, 4)
                own[half, at] = new if first else own[half, at] + new

    def x_copy(c, m=0):
        return remote(hm[m][c], xoth[c], x_s.at[c], x_r.at[c], (f, other))

    def x_send(c):
        for m in range(2):

            @pl.when(core == 1 - m)
            def _():
                x_copy(c, m).start()

    def transpose_x(c):
        for m in range(2):

            @pl.when(core == m)
            def _():
                for s in range(4):
                    mine = hm[m][c][s].reshape(512, 128).astype(F32).T.astype(BF)
                    xt[c, s * 128 : (s + 1) * 128, 0:512] = mine

        x_copy(c).wait_recv()
        for s in range(4):
            theirs = xoth[c][s].reshape(512, 128).astype(F32).T.astype(BF)
            xt[c, s * 128 : (s + 1) * 128, 512:1024] = theirs

    def slope_copy():
        return remote(slope_own, slope_oth, sl_s.at[0], sl_r.at[0], (f, other))

    def h2_copies():
        return [
            remote(
                feat.at[pl.ds(pl.multiple_of(d * 512, 512), 512), pl.ds(0, 256)], hid2_out.at[pl.ds(pl.multiple_of(f * 512, 512), 512)],
                h2_s.at[k], h2_r.at[k], (d, n),
            )
            for k, d in enumerate(far)
        ]

    def along_y(d):
        return (f, z * 8 + ((y + d) % 4) * 2 + core)

    def along_z(d):
        return (f, ((z + d) % 4) * 8 + y * 2 + core)

    def g1_copies(h):
        out = []
        for d in (1, 2, 3):
            if h == 0:
                src, dev = g0.at[:, :, (y + d) % 4], along_y(d)
            else:
                src, dev = g1.at[:, (z + d) % 4], along_z(d)
            out.append(remote(src, r1[h].at[d - 1], g1_s.at[h, d - 1], g1_r.at[h, d - 1], dev))
        return out

    def g2_copies(h):
        out = []
        for d in (1, 2, 3):
            to = (z + d) % 4 if h == 0 else (y + d) % 4
            dev = along_z(d) if h == 0 else along_y(d)
            out.append(remote(s1[h].at[:, to], r2[h].at[d - 1], g2_s.at[h, d - 1], g2_r.at[h, d - 1], dev))
        return out

    def g3_copies(h):
        return [
            remote(
                s2[h].at[(f + d) % 4], r3[h].at[d - 1],
                g3_s.at[h, d - 1], g3_r.at[h, d - 1], ((f + d) % 4, n),
            )
            for d in (1, 2, 3)
        ]

    def fin_copy():
        rows = pl.ds(pl.multiple_of((1 - core) * 8, 8), 8)
        return remote(fin.at[rows], finr, fn_s.at[0], fn_r.at[0], (f, other))

    for c in [*loads, load_mask2]:
        c.wait()
    project(NEIGH, opp, 0)
    start(copies_a(0))
    project(NEIGH, right, 1)
    project(NEIGH, left, 2)
    start(copies_direct(0))
    project(NEIGH, f, None)
    slots_of(0, own1, src1)
    slots_of(1, own2, src2)
    masks_of(0, mask1)
    ring_add(0)
    ring_start(1)
    project(SELF, opp, 0)
    project(SELF, right, 1)
    project(SELF, left, 2)
    project(SELF, f, None)
    masks_of(1, mask2)
    meta_send()
    ring_end(0)
    pieces(0, proj)
    ring_add(1)
    ring_start(2)
    meta_wait()
    build(0)
    ring_end(1)
    pieces(1, proj)
    ring_add(2)
    ring_start(3)
    ring_end(2)
    gather_tiles(0, hid)
    pieces(2, hid)
    rows_send(0, 0, hid)
    ring_add(3)
    ring_end(3)
    gather_tiles(1, hid)
    pieces(3, hid)
    rows_send(0, 1, hid)
    build(1)
    start(cot_copies())
    for k, d in enumerate(far):
        w2_copies(d, k).start()
    rows_wait(0, 0, hid)
    rows_wait(0, 1, hid)
    for k in range(3):
        w2_copies(far[k], k).wait_recv()
    for k, d in enumerate(far):
        w2_forward(d, k).start()
    for k, d in enumerate(far):
        w2_forward(d, k).wait_recv()
    pre_add(0, 0, True)
    pre_add(0, 1, False)
    gather_tiles(2, proj)
    rows_send(1, 0, proj)
    rows_wait(1, 0, proj)
    x_send(0)
    pre_add(1, 0, False)
    transpose_x(0)
    gather_tiles(3, proj)
    rows_send(1, 1, proj)
    for c in cot_copies():
        c.wait_recv()
    rows_wait(1, 1, proj)
    x_send(1)
    pre_add(1, 1, False)
    for j in range(4):

        @pl.loop(0, 4)
        def _(t):
            rows = pl.ds(pl.multiple_of(t * 128, 128), 128)
            out_rows = pl.ds(pl.multiple_of(t * 128 + j * 512, 128), 128)
            for half in range(2):
                cols = slice(half * 128, (half + 1) * 128)
                v = own[half, j * 4 + t]
                s = 1.0 / (1.0 + jnp.exp(-v))
                feat[out_rows, cols] = (v * s).astype(BF)
                up = cot[j, rows, cols].astype(F32) * s * (1.0 + v * (1.0 - s))
                slope_own[j, rows, cols] = up.astype(BF)

    slope_copy().start()
    start(h2_copies())
    mine = pl.ds(pl.multiple_of(f * 512, 512), 512)
    hid2_out[mine, :] = feat[mine, 0:256]
    transpose_x(1)
    slope_copy().wait_recv()
    for j in range(4):
        up = jnp.concatenate([slope_own[j], slope_oth[j]], axis=0)
        grad = g0 if j < 2 else g1
        cols = pl.ds((j % 2) * 256, 256)
        for c in range(2):
            part = dot(xt[c], up).astype(BF)
            grad[:, 2 * c : 2 * c + 2, :, :, cols] = part.reshape(4, 2, 4, 16, 256)
        if j == 1:
            start(g1_copies(0))
        if j == 3:
            start(g1_copies(1))
    for h in range(2):
        for c in g1_copies(h):
            c.wait_recv()
        first = g0[:, :, y] if h == 0 else g1[:, z]
        total = first.astype(F32)
        for d in range(3):
            total = total + r1[h][d].astype(F32)
        s1[h][...] = total
        start(g2_copies(h))
    for h in range(2):
        for c in g2_copies(h):
            c.wait_recv()
        at = z if h == 0 else y
        s2[h][...] = s1[h][:, at] + r2[h][0] + r2[h][1] + r2[h][2]
        start(g3_copies(h))
    for h in range(2):
        for c in g3_copies(h):
            c.wait_recv()
        fin[:, h * 512 : (h + 1) * 512] = s2[h][f] + r3[h][0] + r3[h][1] + r3[h][2]
    fin_copy().start()
    fin_copy().wait_recv()
    mine8 = fin[pl.ds(pl.multiple_of(core * 8, 8), 8), :]
    first_core = jnp.full((8, 1024), core, jnp.int32) == 0
    gs_out[...] = jnp.where(first_core, mine8, finr[...])
    gn_out[...] = jnp.where(first_core, finr[...], mine8)

    for c in h2_copies():
        c.wait_recv()
    for q in range(4):
        for c in copies_a(q) + copies_direct(q) + copies_added(q):
            c.wait_send()

    @pl.loop(1, 32)
    def _(i):
        piece_copy(2, i).wait_send()
        piece_copy(3, i).wait_send()

    for m, values in ((0, hid), (1, proj)):
        for c in range(2):
            for copy in rows_copies(m, c, values):
                copy.wait_send()
    rest = cot_copies() + h2_copies() + [slope_copy(), fin_copy(), x_copy(0), x_copy(1)]
    for k, d in enumerate(far):
        rest += [w2_copies(d, k), w2_forward(d, k)]
    for h in range(2):
        rest += g1_copies(h) + g2_copies(h) + g3_copies(h)
    for copy in rest:
        copy.wait_send()


def local_step(
    features, self_w1, neigh_w1, self_w2, neigh_w2, source_tiles1, owner_blocks1, target_tiles1,
    tile_masks1, source_tiles2, owner_blocks2, target_tiles2, tile_masks2, cotangent,
):
    hbm = pl.BlockSpec(memory_space=pl.ANY)
    smem = pl.BlockSpec(memory_space=pltpu.SMEM)
    vmem = pl.BlockSpec(memory_space=pltpu.VMEM)
    v = pltpu.VMEM
    dma = pltpu.SemaphoreType.DMA

    def pair(*shape):
        return [dma(shape), dma(shape)]

    i32 = jnp.int32
    scratch = [
        v((2048, 512), BF), *[v((512, 1024), BF)] * 2, *[v((32, 128, 128), i32)] * 2,
        v((2, 32, 128, 128), BF), v((2, 32, 8, 128), F32), pltpu.SMEM((2, 32, 8), i32),
        *[v((3, 2048, 128), BF)] * 4, v((4, 16, 128, 128), F32), *[v((2, 1024, 128), BF)] * 4,
        *[v((2, 2048, 128), BF)] * 4, *[v((16, 128, 128), BF)] * 4,
        v((32, 8, 128), F32), v((32, 8, 128), F32), v((1024, 128), F32), v((1024, 128), BF),
        v((2, 256, 1024), BF), v((8, 256, 128), F32),
        *[v((32, 2, 128, 128), BF)] * 6, *[v((4, 4, 128, 128), BF)] * 6, v((2, 512, 1024), BF),
        v((4, 512, 256), BF), v((2, 4, 2, 128, 1024), BF), *[v((4, 512, 256), BF)] * 2,
        *[v((4, 4, 4, 16, 512), BF)] * 2, *[v((3, 4, 4, 16, 512), BF)] * 2,
        *[v((4, 4, 16, 512), F32)] * 2, *[v((3, 4, 16, 512), F32)] * 2, *[v((4, 16, 512), F32)] * 2,
        *[v((3, 16, 512), F32)] * 2, v((16, 1024), F32), v((8, 1024), F32),
        dma((10,)),
        *pair(32), *pair(4, 2), *pair(4, 4), *pair(4, 32), *pair(2, 2, 3), *pair(3), *pair(3),
        *pair(3), *pair(2), *pair(1), *pair(3), *pair(2, 3), *pair(2, 3), *pair(2, 3), *pair(1),
    ]
    hidden2, grad_self, grad_neigh = pl.pallas_call(
        kernel,
        out_shape=(
            jax.ShapeDtypeStruct((2048, 256), BF),
            jax.ShapeDtypeStruct((8, 1024), F32),
            jax.ShapeDtypeStruct((8, 1024), F32),
        ),
        in_specs=[hbm] * 5 + [smem] * 3 + [hbm] + [smem] * 3 + [hbm] * 2,
        out_specs=(vmem, vmem, vmem),
        scratch_shapes=scratch,
        compiler_params=pltpu.CompilerParams(
            collective_id=0, has_side_effects=True, vmem_limit_bytes=(64 << 20) - (64 << 10)
        ),
        cost_estimate=pl.CostEstimate(flops=10**10, bytes_accessed=16 << 20, transcendentals=1 << 19),
        name="sage",
    )(
        features, self_w1, neigh_w1, self_w2, neigh_w2, source_tiles1, owner_blocks1, target_tiles1,
        tile_masks1, source_tiles2, owner_blocks2, target_tiles2, tile_masks2, cotangent,
    )
    return hidden2, grad_self, grad_neigh


def solution(mesh):
    node3 = P("node", None, None)
    in_specs = (
        P("node", "feat"), P("feat", None), P("feat", None), P("feat", None), P("feat", None),
        P("node"), P("node", None), P("node"), node3,
        P("node"), P("node", None), P("node"), node3, P("node", "feat"),
    )
    out_specs = (P("node", "feat"), P(("feat", "node"), None), P(("feat", "node"), None))
    return jax.shard_map(local_step, mesh=mesh, in_specs=in_specs, out_specs=out_specs, check_vma=False)
```

time: 520 us -> 216 us (0.42)
  waiting for transfers between devices: 370 us -> 0 us
  Pallas kernels: 0 us -> 209 us
  matrix products: 51.3 us -> 0 us
  starting transfers between devices: 44 us -> 0 us
  local copies, waits for them, and re-layouts: 28 us -> 6.19 us
  between operations: 14.1 us -> 0.66 us
  other arithmetic: 10.4 us -> 0 us
    reduce_scatter x4 -> x0, waiting for transfers between devices: 223 us -> none  [the longest x1 79.3 us: local(): lax.psum_scatter(jnp.concatenate([lax.dot_general(hidden1, slope_full, co...]
    pallas_call x0 -> x1, Pallas kernels: none -> 209 us  [local_step(): pl.pallas_call(kernel, out_shape=(jax.ShapeDtypeStruct((2048, 256), BF),...]
    all_to_all x6 -> x0, waiting for transfers between devices: 96.8 us -> none  [the longest x1 47.9 us: local(): lax.all_to_all(packed1[0], 'node', split_axis=0, concat_axis=0, tiled=True)]
    dot_general x18 -> x0, matrix products: 51.3 us -> none  [the longest x2 9.79 us: unpack_tiles(): jnp.einsum('st,sx->tx', got_targets, flat_pieces, preferred_element_type=...]
    all_gather x1 -> x0, waiting for transfers between devices: 50.9 us -> none  [local(): slope_full = lax.all_gather(slope, 'feat', axis=1, tiled=True)]
    all_to_all x6 -> x0, starting transfers between devices: 43.5 us -> none  [the longest x1 9.61 us: local(): lax.all_to_all(packed1[2], 'node', split_axis=0, concat_axis=0, tiled=True)]
    unnamed x36 -> x9, local copies, waits for them, and re-layouts: 18 us -> 6.19 us
    convert_element_type x5 -> x0, other arithmetic: 8.17 us -> none  [the longest x1 3.81 us: local(): (cotangent.astype(jnp.float32) * sigma * (1.0 + pre2 * (1.0 - sigma))).as...]
  transfers between devices with their start and end apart: 11 -> 0, of which waited for: 8 -> 0; matrix products, arithmetic and copies ran while one was open for 11% -> 0% of each run, Pallas kernels for 0% -> 0%
where the time goes in v1:
time: 216 us
  Pallas kernels  209 us (97%)
  local copies, waits for them, and re-layouts  6.19 us (3%)
    pallas_call x1, Pallas kernels, local_step(): pl.pallas_call(kernel, out_shape=(jax.ShapeDtypeStruct((2048, 256), BF),...  209 us
    unnamed x9, local copies, waits for them, and re-layouts  6.19 us

profile of v1, /device:TPU:1, one launch (start us, length us, event | category | flops | bytes accessed | tf_op | source)
XLA Modules:
  0.0 215.8 jit_solution(16680210940206547239)
XLA Ops:
  0.6 1.3 copy.17.own1
  2.0 1.3 copy.18.own2
  3.3 209.0 %sage.1 = (bf16[2048,256]{1,0:T(8,128)(2,1)}, f32[8,1024]{1,0:T(8,128)}, f32[8,1024]{1,0:T(8,128)}) custom-call(bf16[2048,512]{1,0:T(8,128)(2,1)} %feat_hbm.1, bf16[512,1024]{1,0:T(8,128)(2,1)} %ws1_hbm.1, bf16[512,1024]{1,0:T(8,128)(2,1)} %wn1_hbm.1, bf16[256,1024]{1,0:T(8,128)(2,1)} %ws2_hbm.1, bf16[256,1024]{1,0:T(8,128)(2,1)} %wn2_hbm.1, s32[32]{0:T(128)} %src1.1, ...), custom_call_target="tpu_custom_call" | custom-call | flops 10000000000 | bytes 16777216 | tf_op jit(solution)/shard_map/sage/pallas_call | solution.py:572
  212.3 0.0 copy-start.1
  212.3 0.0 copy-start
  212.3 2.3 %copy.22 = bf16[2048,256]{1,0:T(8,128)(2,1)} copy(bf16[2048,256]{1,0:T(8,128)(2,1)} %get-tuple-element.6) | data formatting | bytes 2097152
  214.6 0.0 copy-done.1
  214.6 0.6 copy.23
  215.2 0.0 copy-done
  215.2 0.6 copy.24
Async XLA Ops:
  212.3 2.3 %copy-start.1 = (f32[8,1024]{1,0:T(8,128)S(1)}, f32[8,1024]{1,0:T(8,128)}, u32[]{:S(2)}) copy-start(f32[8,1024]{1,0:T(8,128)} %get-tuple-element.7) | copy-start | bytes 98308
  212.3 2.9 %copy-start = (f32[8,1024]{1,0:T(8,128)S(1)}, f32[8,1024]{1,0:T(8,128)}, u32[]{:S(2)}) copy-start(f32[8,1024]{1,0:T(8,128)} %get-tuple-element.8) | copy-start | bytes 98308

commit v2 on v1

--- a/solution.py
+++ b/solution.py
@@ -19,7 +19,7 @@
 
 def kernel(
     feat_hbm, ws1_hbm, wn1_hbm, ws2_hbm, wn2_hbm,
-    src1, own1, tgt1, mask1_hbm, src2, own2, tgt2, mask2_hbm, cot_hbm,
+    src1, tgt1, mask1_hbm, src2, tgt2, mask2_hbm, owners, cot_hbm,
     hid2_out, gs_out, gn_out,
     feat, w1n, w1s, mask1, mask2, maskt, cnt, tab,
     p0, p1, p2, p3, own, a0, a1, a2, a3, b0, b1, b2, b3, proj0, proj1, hid0, hid1,
@@ -119,10 +119,6 @@
         for c in copies:
             c.start()
 
-    def ring_start(q):
-        start(copies_a(q))
-        start(copies_direct(q))
-
     def ring_add(q):
         a, b = copies_a(q), copies_added(q)
         for s, base in ((0, 0), (1, 1024)):
@@ -158,14 +154,14 @@
             cnt[layer, e] = jnp.broadcast_to(jnp.sum(m, axis=0, keepdims=True), (8, 128))
             maskt[layer, e] = m.T.astype(BF)
 
-    def slots_of(layer, owners, sources):
+    def slots_of(layer, sources):
         @pl.loop(0, 32)
         def _(i):
             who = peer(i)[1]
 
             def look(e, carry):
                 seen, first, second = carry
-                hit = owners[e, 0] == who
+                hit = owners[layer * 32 + e] == who
                 first = jnp.where(jnp.logical_and(hit, seen == 0), e, first)
                 second = jnp.where(jnp.logical_and(hit, seen == 1), e, second)
                 return seen + hit.astype(jnp.int32), first, second
@@ -393,54 +389,60 @@
         rows = pl.ds(pl.multiple_of((1 - core) * 8, 8), 8)
         return remote(fin.at[rows], finr, fn_s.at[0], fn_r.at[0], (f, other))
 
-    for c in [*loads, load_mask2]:
-        c.wait()
+    loads[0].wait()
+    loads[1].wait()
     project(NEIGH, opp, 0)
     start(copies_a(0))
     project(NEIGH, right, 1)
     project(NEIGH, left, 2)
     start(copies_direct(0))
+    start(copies_a(1))
     project(NEIGH, f, None)
-    slots_of(0, own1, src1)
-    slots_of(1, own2, src2)
+    for c in loads[2:]:
+        c.wait()
     masks_of(0, mask1)
     ring_add(0)
-    ring_start(1)
+    start(copies_direct(1))
+    slots_of(0, src1)
     project(SELF, opp, 0)
+    ring_add(1)
+    start(copies_a(2))
     project(SELF, right, 1)
     project(SELF, left, 2)
+    start(copies_direct(2))
     project(SELF, f, None)
-    masks_of(1, mask2)
-    meta_send()
     ring_end(0)
     pieces(0, proj)
-    ring_add(1)
-    ring_start(2)
-    meta_wait()
-    build(0)
+    load_mask2.wait()
+    masks_of(1, mask2)
+    slots_of(1, src2)
+    meta_send()
+    start(copies_a(3))
     ring_end(1)
     pieces(1, proj)
     ring_add(2)
-    ring_start(3)
+    start(copies_direct(3))
+    meta_wait()
+    build(0)
+    ring_add(3)
     ring_end(2)
     gather_tiles(0, hid)
     pieces(2, hid)
     rows_send(0, 0, hid)
-    ring_add(3)
+    for k, d in enumerate(far):
+        w2_copies(d, k).start()
+    start(cot_copies())
     ring_end(3)
     gather_tiles(1, hid)
     pieces(3, hid)
     rows_send(0, 1, hid)
     build(1)
-    start(cot_copies())
-    for k, d in enumerate(far):
-        w2_copies(d, k).start()
-    rows_wait(0, 0, hid)
-    rows_wait(0, 1, hid)
     for k in range(3):
         w2_copies(far[k], k).wait_recv()
     for k, d in enumerate(far):
         w2_forward(d, k).start()
+    rows_wait(0, 0, hid)
+    rows_wait(0, 1, hid)
     for k, d in enumerate(far):
         w2_forward(d, k).wait_recv()
     pre_add(0, 0, True)
@@ -576,7 +578,7 @@
             jax.ShapeDtypeStruct((8, 1024), F32),
             jax.ShapeDtypeStruct((8, 1024), F32),
         ),
-        in_specs=[hbm] * 5 + [smem] * 3 + [hbm] + [smem] * 3 + [hbm] * 2,
+        in_specs=[hbm] * 5 + [smem] * 2 + [hbm] + [smem] * 2 + [hbm, smem, hbm],
         out_specs=(vmem, vmem, vmem),
         scratch_shapes=scratch,
         compiler_params=pltpu.CompilerParams(
@@ -585,8 +587,9 @@
         cost_estimate=pl.CostEstimate(flops=10**10, bytes_accessed=16 << 20, transcendentals=1 << 19),
         name="sage",
     )(
-        features, self_w1, neigh_w1, self_w2, neigh_w2, source_tiles1, owner_blocks1, target_tiles1,
-        tile_masks1, source_tiles2, owner_blocks2, target_tiles2, tile_masks2, cotangent,
+        features, self_w1, neigh_w1, self_w2, neigh_w2, source_tiles1, target_tiles1, tile_masks1,
+        source_tiles2, target_tiles2, tile_masks2,
+        jnp.concatenate([owner_blocks1[:, 0], owner_blocks2[:, 0]]), cotangent,
     )
     return hidden2, grad_self, grad_neigh
 

time: 216 us -> 202 us (0.935)
  Pallas kernels: 209 us -> 196 us
  local copies, waits for them, and re-layouts: 6.19 us -> 3.51 us
    pallas_call x1, Pallas kernels: 209 us -> 196 us  [local_step(): pl.pallas_call(kernel, out_shape=(jax.ShapeDtypeStruct((2048, 256), BF),...]
    unnamed x9 -> x7, local copies, waits for them, and re-layouts: 6.19 us -> 3.51 us
where the time goes in v2:
time: 202 us; the launch traced here: 201 us
  Pallas kernels  196 us (97%)
  local copies, waits for them, and re-layouts  3.51 us (2%)
    pallas_call x1, Pallas kernels, local_step(): pl.pallas_call(kernel, out_shape=(jax.ShapeDtypeStruct((2048, 256), BF),...  196 us

profile of v2, /device:TPU:1, one launch (start us, length us, event | category | flops | bytes accessed | tf_op | source)
XLA Modules:
  0.0 201.4 jit_solution(719886766868996434)
XLA Ops:
  0.6 1.3 pad_add_fusion.owners
  1.9 196.0 %sage.1 = (bf16[2048,256]{1,0:T(8,128)(2,1)}, f32[8,1024]{1,0:T(8,128)}, f32[8,1024]{1,0:T(8,128)}) custom-call(bf16[2048,512]{1,0:T(8,128)(2,1)} %feat_hbm.1, bf16[512,1024]{1,0:T(8,128)(2,1)} %ws1_hbm.1, bf16[512,1024]{1,0:T(8,128)(2,1)} %wn1_hbm.1, bf16[256,1024]{1,0:T(8,128)(2,1)} %ws2_hbm.1, bf16[256,1024]{1,0:T(8,128)(2,1)} %wn2_hbm.1, s32[32]{0:T(128)} %src1.1, ...), custom_call_target="tpu_custom_call" | custom-call | flops 10000000000 | bytes 16777216 | tf_op jit(solution)/shard_map/sage/pallas_call | solution.py:574
  197.9 0.0 copy-start.1
  197.9 0.0 copy-start
  197.9 2.3 %copy.20 = bf16[2048,256]{1,0:T(8,128)(2,1)} copy(bf16[2048,256]{1,0:T(8,128)(2,1)} %get-tuple-element.6) | data formatting | bytes 2097152
  200.2 0.0 copy-done.1
  200.2 0.6 copy.21
  200.8 0.0 copy-done
  200.8 0.6 copy.22
Async XLA Ops:
  197.9 2.3 %copy-start.1 = (f32[8,1024]{1,0:T(8,128)S(1)}, f32[8,1024]{1,0:T(8,128)}, u32[]{:S(2)}) copy-start(f32[8,1024]{1,0:T(8,128)} %get-tuple-element.7) | copy-start | bytes 98308
  197.9 2.9 %copy-start = (f32[8,1024]{1,0:T(8,128)S(1)}, f32[8,1024]{1,0:T(8,128)}, u32[]{:S(2)}) copy-start(f32[8,1024]{1,0:T(8,128)} %get-tuple-element.8) | copy-start | bytes 98308

commit v3 on v2

--- a/solution.py
+++ b/solution.py
@@ -25,10 +25,10 @@
     p0, p1, p2, p3, own, a0, a1, a2, a3, b0, b1, b2, b3, proj0, proj1, hid0, hid1,
     msg_out, msg_in, vcol, ccol, lhs, rdeg,
     send0, send1, recv0, recv1, recv2, recv3, h0, h1, m0, m1, xoth0, xoth1, xt,
-    cot, w2, slope_own, slope_oth,
+    cot, w2, wx, slope_own, slope_oth,
     g0, g1, r1a, r1b, s1a, s1b, r2a, r2b, s2a, s2b, r3a, r3b, fin, finr,
     ld, meta_s, meta_r, ra_s, ra_r, rb_s, rb_r, aa_s, aa_r, rows_s, rows_r,
-    cot_s, cot_r, w2_s, w2_r, wd_s, wd_r, x_s, x_r, sl_s, sl_r, h2_s, h2_r,
+    cot_s, cot_r, w2_s, w2_r, ws_s, ws_r, wd_s, wd_r, x_s, x_r, sl_s, sl_r, h2_s, h2_r,
     g1_s, g1_r, g2_s, g2_r, g3_s, g3_r, fn_s, fn_r,
 ):
     f = lax.axis_index("feat")
@@ -65,8 +65,7 @@
         local(cot_hbm.at[pl.ds(pl.multiple_of(f * 512, 512), 512)], cot.at[f], 4),
     ]
     for m, ref in ((0, ws2_hbm), (1, wn2_hbm)):
-        for c in range(2):
-            loads.append(local(ref.at[pl.ds(c * 128, 128)], w2.at[m, f, c], 5 + 2 * m + c))
+        loads.append(local(ref, w2.at[m, f], 5 + m))
     load_mask2 = local(mask2_hbm, mask2, 9)
     for c in [*loads, load_mask2]:
         c.start()
@@ -266,7 +265,6 @@
             result[c][:, rows, :] = mean.astype(BF).reshape(16, 16, 128)
 
     far = (right, left, opp)
-    back = (1, 0, 2)
 
     def rows_copies(m, c, values):
         return [
@@ -294,10 +292,22 @@
             for k, d in enumerate(far)
         ]
 
-    def w2_copies(d, k):
-        return remote(
-            w2.at[core, f], w2.at[core, f], w2_s.at[k], w2_r.at[k], (d, n)
-        )
+    back = (left, right, opp)
+    chip = z * 4 + y
+
+    def w2_first(k, m=0):
+        rows = pl.ds(pl.multiple_of(chip * 16, 16), 16)
+        src = (ws2_hbm, wn2_hbm)[m].at[rows]
+        return remote(src, wx.at[k], w2_s.at[k], w2_r.at[k], (far[k], n))
+
+    def w2_place(k):
+        return w2.at[core, back[k], pl.ds(pl.multiple_of(chip * 16, 16), 16)]
+
+    def w2_spread(i, k):
+        zz = (z + sign * (i // 4) + 4) % 4
+        yy = (y + sign * (i % 4) + 4) % 4
+        dev = (f, zz * 8 + yy * 2 + core)
+        return remote(wx.at[k], w2_place(k), ws_s.at[i, k], ws_r.at[i, k], dev)
 
     def w2_forward(d, k):
         return remote(
@@ -310,7 +320,7 @@
         @pl.loop(0, 4)
         def _(j):
             cols = pl.ds(pl.multiple_of(j * 256, 256), 256)
-            part = dot(left_side, w2[m, :, c, :, cols].reshape(512, 256))
+            part = dot(left_side, w2[m, :, c * 128 : (c + 1) * 128, cols].reshape(512, 256))
             for half in range(2):
                 new = part[:, half * 128 : (half + 1) * 128].reshape(4, 128, 128)
                 at = pl.ds(j * 4, 4)
@@ -389,6 +399,13 @@
         rows = pl.ds(pl.multiple_of((1 - core) * 8, 8), 8)
         return remote(fin.at[rows], finr, fn_s.at[0], fn_r.at[0], (f, other))
 
+    for m in range(2):
+
+        @pl.when(core == m)
+        def _():
+            for k in range(3):
+                w2_first(k, m).start()
+
     loads[0].wait()
     loads[1].wait()
     project(NEIGH, opp, 0)
@@ -396,23 +413,33 @@
     project(NEIGH, right, 1)
     project(NEIGH, left, 2)
     start(copies_direct(0))
-    start(copies_a(1))
     project(NEIGH, f, None)
     for c in loads[2:]:
         c.wait()
+    for k in range(3):
+        w2_first(k).wait_recv()
+
+    @pl.loop(1, 16)
+    def _(i):
+        for k in range(3):
+            w2_spread(i, k).start()
+
+    for k in range(3):
+        local(wx.at[k], w2_place(k), 10 + k).start()
+    ring_add(0)
+    start(copies_a(1))
+    start(copies_direct(1))
     masks_of(0, mask1)
-    ring_add(0)
-    start(copies_direct(1))
     slots_of(0, src1)
     project(SELF, opp, 0)
+    project(SELF, right, 1)
+    project(SELF, left, 2)
+    ring_end(0)
+    pieces(0, proj)
     ring_add(1)
     start(copies_a(2))
-    project(SELF, right, 1)
-    project(SELF, left, 2)
     start(copies_direct(2))
     project(SELF, f, None)
-    ring_end(0)
-    pieces(0, proj)
     load_mask2.wait()
     masks_of(1, mask2)
     slots_of(1, src2)
@@ -425,22 +452,26 @@
     meta_wait()
     build(0)
     ring_add(3)
+
+    @pl.loop(1, 16)
+    def _(i):
+        for k in range(3):
+            w2_spread(i, k).wait_recv()
+
+    for k in range(3):
+        local(wx.at[k], w2_place(k), 10 + k).wait()
+    for k, d in enumerate(far):
+        w2_forward(d, k).start()
     ring_end(2)
     gather_tiles(0, hid)
     pieces(2, hid)
     rows_send(0, 0, hid)
-    for k, d in enumerate(far):
-        w2_copies(d, k).start()
     start(cot_copies())
     ring_end(3)
     gather_tiles(1, hid)
     pieces(3, hid)
     rows_send(0, 1, hid)
     build(1)
-    for k in range(3):
-        w2_copies(far[k], k).wait_recv()
-    for k, d in enumerate(far):
-        w2_forward(d, k).start()
     rows_wait(0, 0, hid)
     rows_wait(0, 1, hid)
     for k, d in enumerate(far):
@@ -523,6 +554,11 @@
         for c in copies_a(q) + copies_direct(q) + copies_added(q):
             c.wait_send()
 
+    @pl.loop(1, 16)
+    def _(i):
+        for k in range(3):
+            w2_spread(i, k).wait_send()
+
     @pl.loop(1, 32)
     def _(i):
         piece_copy(2, i).wait_send()
@@ -534,7 +570,7 @@
                 copy.wait_send()
     rest = cot_copies() + h2_copies() + [slope_copy(), fin_copy(), x_copy(0), x_copy(1)]
     for k, d in enumerate(far):
-        rest += [w2_copies(d, k), w2_forward(d, k)]
+        rest += [w2_first(k), w2_forward(d, k)]
     for h in range(2):
         rest += g1_copies(h) + g2_copies(h) + g3_copies(h)
     for copy in rest:
@@ -563,13 +599,13 @@
         v((32, 8, 128), F32), v((32, 8, 128), F32), v((1024, 128), F32), v((1024, 128), BF),
         v((2, 256, 1024), BF), v((8, 256, 128), F32),
         *[v((32, 2, 128, 128), BF)] * 6, *[v((4, 4, 128, 128), BF)] * 6, v((2, 512, 1024), BF),
-        v((4, 512, 256), BF), v((2, 4, 2, 128, 1024), BF), *[v((4, 512, 256), BF)] * 2,
+        v((4, 512, 256), BF), v((2, 4, 256, 1024), BF), v((3, 16, 1024), BF), *[v((4, 512, 256), BF)] * 2,
         *[v((4, 4, 4, 16, 512), BF)] * 2, *[v((3, 4, 4, 16, 512), BF)] * 2,
         *[v((4, 4, 16, 512), F32)] * 2, *[v((3, 4, 16, 512), F32)] * 2, *[v((4, 16, 512), F32)] * 2,
         *[v((3, 16, 512), F32)] * 2, v((16, 1024), F32), v((8, 1024), F32),
-        dma((10,)),
+        dma((13,)),
         *pair(32), *pair(4, 2), *pair(4, 4), *pair(4, 32), *pair(2, 2, 3), *pair(3), *pair(3),
-        *pair(3), *pair(2), *pair(1), *pair(3), *pair(2, 3), *pair(2, 3), *pair(2, 3), *pair(1),
+        *pair(16, 3), *pair(3), *pair(2), *pair(1), *pair(3), *pair(2, 3), *pair(2, 3), *pair(2, 3), *pair(1),
     ]
     hidden2, grad_self, grad_neigh = pl.pallas_call(
         kernel,

time: 202 us -> 200 us (0.990)
  no operation moved by 1% of the time
where the time goes in v3:
time: 200 us
  Pallas kernels  195 us (98%)
  local copies, waits for them, and re-layouts  3.51 us (2%)
    pallas_call x1, Pallas kernels, local_step(): pl.pallas_call(kernel, out_shape=(jax.ShapeDtypeStruct((2048, 256), BF),...  195 us

profile of v3, /device:TPU:1, one launch (start us, length us, event | category | flops | bytes accessed | tf_op | source)
XLA Modules:
  0.0 200.3 jit_solution(12539537344375397080)
XLA Ops:
  0.6 1.3 pad_add_fusion.owners
  1.9 194.9 %sage.1 = (bf16[2048,256]{1,0:T(8,128)(2,1)}, f32[8,1024]{1,0:T(8,128)}, f32[8,1024]{1,0:T(8,128)}) custom-call(bf16[2048,512]{1,0:T(8,128)(2,1)} %feat_hbm.1, bf16[512,1024]{1,0:T(8,128)(2,1)} %ws1_hbm.1, bf16[512,1024]{1,0:T(8,128)(2,1)} %wn1_hbm.1, bf16[256,1024]{1,0:T(8,128)(2,1)} %ws2_hbm.1, bf16[256,1024]{1,0:T(8,128)(2,1)} %wn2_hbm.1, s32[32]{0:T(128)} %src1.1, ...), custom_call_target="tpu_custom_call" | custom-call | flops 10000000000 | bytes 16777216 | tf_op jit(solution)/shard_map/sage/pallas_call | solution.py:610
  196.8 0.0 copy-start.1
  196.8 0.0 copy-start
  196.8 2.3 %copy.20 = bf16[2048,256]{1,0:T(8,128)(2,1)} copy(bf16[2048,256]{1,0:T(8,128)(2,1)} %get-tuple-element.6) | data formatting | bytes 2097152
  199.1 0.0 copy-done.1
  199.1 0.6 copy.21
  199.7 0.0 copy-done
  199.7 0.6 copy.22
Async XLA Ops:
  196.8 2.3 %copy-start.1 = (f32[8,1024]{1,0:T(8,128)S(1)}, f32[8,1024]{1,0:T(8,128)}, u32[]{:S(2)}) copy-start(f32[8,1024]{1,0:T(8,128)} %get-tuple-element.7) | copy-start | bytes 98308
  196.8 2.9 %copy-start = (f32[8,1024]{1,0:T(8,128)S(1)}, f32[8,1024]{1,0:T(8,128)}, u32[]{:S(2)}) copy-start(f32[8,1024]{1,0:T(8,128)} %get-tuple-element.8) | copy-start | bytes 98308

commit v4 on v3

--- a/solution.py
+++ b/solution.py
@@ -292,22 +292,24 @@
             for k, d in enumerate(far)
         ]
 
-    back = (left, right, opp)
     chip = z * 4 + y
-
-    def w2_first(k, m=0):
-        rows = pl.ds(pl.multiple_of(chip * 16, 16), 16)
-        src = (ws2_hbm, wn2_hbm)[m].at[rows]
-        return remote(src, wx.at[k], w2_s.at[k], w2_r.at[k], (far[k], n))
-
-    def w2_place(k):
-        return w2.at[core, back[k], pl.ds(pl.multiple_of(chip * 16, 16), 16)]
-
-    def w2_spread(i, k):
+    slice_rows = pl.ds(pl.multiple_of(chip * 16, 16), 16)
+
+    def w2_near(k):
+        return remote(w2.at[core, f], w2.at[core, f], w2_s.at[k], w2_r.at[k], (far[k], n))
+
+    def w2_first(m=0):
+        src = (ws2_hbm, wn2_hbm)[m].at[slice_rows]
+        return remote(src, wx, w2_s.at[2], w2_r.at[2], (opp, n))
+
+    def w2_own():
+        return local(wx, w2.at[core, opp, slice_rows], 10)
+
+    def w2_spread(i):
         zz = (z + sign * (i // 4) + 4) % 4
         yy = (y + sign * (i % 4) + 4) % 4
         dev = (f, zz * 8 + yy * 2 + core)
-        return remote(wx.at[k], w2_place(k), ws_s.at[i, k], ws_r.at[i, k], dev)
+        return remote(wx, w2.at[core, opp, slice_rows], ws_s.at[i], ws_r.at[i], dev)
 
     def w2_forward(d, k):
         return remote(
@@ -403,8 +405,7 @@
 
         @pl.when(core == m)
         def _():
-            for k in range(3):
-                w2_first(k, m).start()
+            w2_first(m).start()
 
     loads[0].wait()
     loads[1].wait()
@@ -416,16 +417,13 @@
     project(NEIGH, f, None)
     for c in loads[2:]:
         c.wait()
-    for k in range(3):
-        w2_first(k).wait_recv()
+    w2_first().wait_recv()
 
     @pl.loop(1, 16)
     def _(i):
-        for k in range(3):
-            w2_spread(i, k).start()
-
-    for k in range(3):
-        local(wx.at[k], w2_place(k), 10 + k).start()
+        w2_spread(i).start()
+
+    w2_own().start()
     ring_add(0)
     start(copies_a(1))
     start(copies_direct(1))
@@ -453,15 +451,8 @@
     build(0)
     ring_add(3)
 
-    @pl.loop(1, 16)
-    def _(i):
-        for k in range(3):
-            w2_spread(i, k).wait_recv()
-
-    for k in range(3):
-        local(wx.at[k], w2_place(k), 10 + k).wait()
-    for k, d in enumerate(far):
-        w2_forward(d, k).start()
+    for k in range(2):
+        w2_near(k).start()
     ring_end(2)
     gather_tiles(0, hid)
     pieces(2, hid)
@@ -471,7 +462,17 @@
     gather_tiles(1, hid)
     pieces(3, hid)
     rows_send(0, 1, hid)
+    w2_own().wait()
+
+    @pl.loop(1, 16)
+    def _(i):
+        w2_spread(i).wait_recv()
+
     build(1)
+    for k in range(2):
+        w2_near(k).wait_recv()
+    for k, d in enumerate(far):
+        w2_forward(d, k).start()
     rows_wait(0, 0, hid)
     rows_wait(0, 1, hid)
     for k, d in enumerate(far):
@@ -556,8 +557,7 @@
 
     @pl.loop(1, 16)
     def _(i):
-        for k in range(3):
-            w2_spread(i, k).wait_send()
+        w2_spread(i).wait_send()
 
     @pl.loop(1, 32)
     def _(i):
@@ -569,8 +569,7 @@
             for copy in rows_copies(m, c, values):
                 copy.wait_send()
     rest = cot_copies() + h2_copies() + [slope_copy(), fin_copy(), x_copy(0), x_copy(1)]
-    for k, d in enumerate(far):
-        rest += [w2_first(k), w2_forward(d, k)]
+    rest += [w2_near(0), w2_near(1), w2_first()] + [w2_forward(d, k) for k, d in enumerate(far)]
     for h in range(2):
         rest += g1_copies(h) + g2_copies(h) + g3_copies(h)
     for copy in rest:
@@ -599,13 +598,13 @@
         v((32, 8, 128), F32), v((32, 8, 128), F32), v((1024, 128), F32), v((1024, 128), BF),
         v((2, 256, 1024), BF), v((8, 256, 128), F32),
         *[v((32, 2, 128, 128), BF)] * 6, *[v((4, 4, 128, 128), BF)] * 6, v((2, 512, 1024), BF),
-        v((4, 512, 256), BF), v((2, 4, 256, 1024), BF), v((3, 16, 1024), BF), *[v((4, 512, 256), BF)] * 2,
+        v((4, 512, 256), BF), v((2, 4, 256, 1024), BF), v((16, 1024), BF), *[v((4, 512, 256), BF)] * 2,
         *[v((4, 4, 4, 16, 512), BF)] * 2, *[v((3, 4, 4, 16, 512), BF)] * 2,
         *[v((4, 4, 16, 512), F32)] * 2, *[v((3, 4, 16, 512), F32)] * 2, *[v((4, 16, 512), F32)] * 2,
         *[v((3, 16, 512), F32)] * 2, v((16, 1024), F32), v((8, 1024), F32),
-        dma((13,)),
+        dma((11,)),
         *pair(32), *pair(4, 2), *pair(4, 4), *pair(4, 32), *pair(2, 2, 3), *pair(3), *pair(3),
-        *pair(16, 3), *pair(3), *pair(2), *pair(1), *pair(3), *pair(2, 3), *pair(2, 3), *pair(2, 3), *pair(1),
+        *pair(16), *pair(3), *pair(2), *pair(1), *pair(3), *pair(2, 3), *pair(2, 3), *pair(2, 3), *pair(1),
     ]
     hidden2, grad_self, grad_neigh = pl.pallas_call(
         kernel,

time: 200 us -> 188 us (0.940)
  Pallas kernels: 195 us -> 182 us
    pallas_call x1, Pallas kernels: 195 us -> 182 us  [local_step(): pl.pallas_call(kernel, out_shape=(jax.ShapeDtypeStruct((2048, 256), BF),...]
where the time goes in v4:
time: 188 us
  Pallas kernels  182 us (97%)
  local copies, waits for them, and re-layouts  3.51 us (2%)
    pallas_call x1, Pallas kernels, local_step(): pl.pallas_call(kernel, out_shape=(jax.ShapeDtypeStruct((2048, 256), BF),...  182 us

profile of v4, /device:TPU:1, one launch (start us, length us, event | category | flops | bytes accessed | tf_op | source)
XLA Modules:
  0.0 187.8 jit_solution(13784854139690839105)
XLA Ops:
  0.6 1.3 pad_add_fusion.owners
  1.9 182.3 %sage.1 = (bf16[2048,256]{1,0:T(8,128)(2,1)}, f32[8,1024]{1,0:T(8,128)}, f32[8,1024]{1,0:T(8,128)}) custom-call(bf16[2048,512]{1,0:T(8,128)(2,1)} %feat_hbm.1, bf16[512,1024]{1,0:T(8,128)(2,1)} %ws1_hbm.1, bf16[512,1024]{1,0:T(8,128)(2,1)} %wn1_hbm.1, bf16[256,1024]{1,0:T(8,128)(2,1)} %ws2_hbm.1, bf16[256,1024]{1,0:T(8,128)(2,1)} %wn2_hbm.1, s32[32]{0:T(128)} %src1.1, ...), custom_call_target="tpu_custom_call" | custom-call | flops 10000000000 | bytes 16777216 | tf_op jit(solution)/shard_map/sage/pallas_call | solution.py:609
  184.2 0.0 copy-start.1
  184.2 0.0 copy-start
  184.3 2.3 %copy.20 = bf16[2048,256]{1,0:T(8,128)(2,1)} copy(bf16[2048,256]{1,0:T(8,128)(2,1)} %get-tuple-element.6) | data formatting | bytes 2097152
  186.5 0.0 copy-done.1
  186.5 0.6 copy.21
  187.1 0.0 copy-done
  187.2 0.6 copy.22
Async XLA Ops:
  184.2 2.3 %copy-start.1 = (f32[8,1024]{1,0:T(8,128)S(1)}, f32[8,1024]{1,0:T(8,128)}, u32[]{:S(2)}) copy-start(f32[8,1024]{1,0:T(8,128)} %get-tuple-element.7) | copy-start | bytes 98308
  184.2 2.9 %copy-start = (f32[8,1024]{1,0:T(8,128)S(1)}, f32[8,1024]{1,0:T(8,128)}, u32[]{:S(2)}) copy-start(f32[8,1024]{1,0:T(8,128)} %get-tuple-element.8) | copy-start | bytes 98308

commit v5 on v4

--- a/solution.py
+++ b/solution.py
@@ -430,12 +430,12 @@
     masks_of(0, mask1)
     slots_of(0, src1)
     project(SELF, opp, 0)
-    project(SELF, right, 1)
-    project(SELF, left, 2)
     ring_end(0)
     pieces(0, proj)
     ring_add(1)
     start(copies_a(2))
+    project(SELF, right, 1)
+    project(SELF, left, 2)
     start(copies_direct(2))
     project(SELF, f, None)
     load_mask2.wait()

time: 188 us -> 187 us (level)
  no operation moved by 1% of the time
where the time goes in v5:
time: 187 us
  Pallas kernels  182 us (97%)
  local copies, waits for them, and re-layouts  3.51 us (2%)
    pallas_call x1, Pallas kernels, local_step(): pl.pallas_call(kernel, out_shape=(jax.ShapeDtypeStruct((2048, 256), BF),...  182 us

profile of v5, /device:TPU:1, one launch (start us, length us, event | category | flops | bytes accessed | tf_op | source)
XLA Modules:
  0.0 187.0 jit_solution(14495963335508517158)
XLA Ops:
  0.6 1.3 pad_add_fusion.owners
  1.9 181.5 %sage.1 = (bf16[2048,256]{1,0:T(8,128)(2,1)}, f32[8,1024]{1,0:T(8,128)}, f32[8,1024]{1,0:T(8,128)}) custom-call(bf16[2048,512]{1,0:T(8,128)(2,1)} %feat_hbm.1, bf16[512,1024]{1,0:T(8,128)(2,1)} %ws1_hbm.1, bf16[512,1024]{1,0:T(8,128)(2,1)} %wn1_hbm.1, bf16[256,1024]{1,0:T(8,128)(2,1)} %ws2_hbm.1, bf16[256,1024]{1,0:T(8,128)(2,1)} %wn2_hbm.1, s32[32]{0:T(128)} %src1.1, ...), custom_call_target="tpu_custom_call" | custom-call | flops 10000000000 | bytes 16777216 | tf_op jit(solution)/shard_map/sage/pallas_call | solution.py:609
  183.4 0.0 copy-start.1
  183.4 0.0 copy-start
  183.4 2.3 %copy.20 = bf16[2048,256]{1,0:T(8,128)(2,1)} copy(bf16[2048,256]{1,0:T(8,128)(2,1)} %get-tuple-element.6) | data formatting | bytes 2097152
  185.7 0.0 copy-done.1
  185.7 0.6 copy.21
  186.3 0.0 copy-done
  186.3 0.6 copy.22
Async XLA Ops:
  183.4 2.3 %copy-start.1 = (f32[8,1024]{1,0:T(8,128)S(1)}, f32[8,1024]{1,0:T(8,128)}, u32[]{:S(2)}) copy-start(f32[8,1024]{1,0:T(8,128)} %get-tuple-element.7) | copy-start | bytes 98308
  183.4 2.9 %copy-start = (f32[8,1024]{1,0:T(8,128)S(1)}, f32[8,1024]{1,0:T(8,128)}, u32[]{:S(2)}) copy-start(f32[8,1024]{1,0:T(8,128)} %get-tuple-element.8) | copy-start | bytes 98308

commit v6 on v5

--- a/solution.py
+++ b/solution.py
@@ -25,7 +25,7 @@
     p0, p1, p2, p3, own, a0, a1, a2, a3, b0, b1, b2, b3, proj0, proj1, hid0, hid1,
     msg_out, msg_in, vcol, ccol, lhs, rdeg,
     send0, send1, recv0, recv1, recv2, recv3, h0, h1, m0, m1, xoth0, xoth1, xt,
-    cot, w2, wx, slope_own, slope_oth,
+    cot, w2, wx, u0, u1, u2, u3, o0, o1, o2, o3,
     g0, g1, r1a, r1b, s1a, s1b, r2a, r2b, s2a, s2b, r3a, r3b, fin, finr,
     ld, meta_s, meta_r, ra_s, ra_r, rb_s, rb_r, aa_s, aa_r, rows_s, rows_r,
     cot_s, cot_r, w2_s, w2_r, ws_s, ws_r, wd_s, wd_r, x_s, x_r, sl_s, sl_r, h2_s, h2_r,
@@ -41,6 +41,7 @@
     psend, buf_a, buf_b = (p0, p1, p2, p3), (a0, a1, a2, a3), (b0, b1, b2, b3)
     sendbuf, recv = (send0, send1), (recv0, recv1, recv2, recv3)
     hm, xoth = ((h0, h1), (m0, m1)), (xoth0, xoth1)
+    slope_own, slope_oth = (u0, u1, u2, u3), (o0, o1, o2, o3)
     r1, s1, r2, s2, r3 = (r1a, r1b), (s1a, s1b), (r2a, r2b), (s2a, s2b), (r3a, r3b)
 
     def peer(i):
@@ -352,8 +353,8 @@
             theirs = xoth[c][s].reshape(512, 128).astype(F32).T.astype(BF)
             xt[c, s * 128 : (s + 1) * 128, 512:1024] = theirs
 
-    def slope_copy():
-        return remote(slope_own, slope_oth, sl_s.at[0], sl_r.at[0], (f, other))
+    def slope_copy(j):
+        return remote(slope_own[j], slope_oth[j], sl_s.at[j], sl_r.at[j], (f, other))
 
     def h2_copies():
         return [
@@ -504,16 +505,17 @@
                 s = 1.0 / (1.0 + jnp.exp(-v))
                 feat[out_rows, cols] = (v * s).astype(BF)
                 up = cot[j, rows, cols].astype(F32) * s * (1.0 + v * (1.0 - s))
-                slope_own[j, rows, cols] = up.astype(BF)
-
-    slope_copy().start()
+                slope_own[j][rows, cols] = up.astype(BF)
+
+        slope_copy(j).start()
+
     start(h2_copies())
     mine = pl.ds(pl.multiple_of(f * 512, 512), 512)
     hid2_out[mine, :] = feat[mine, 0:256]
     transpose_x(1)
-    slope_copy().wait_recv()
     for j in range(4):
-        up = jnp.concatenate([slope_own[j], slope_oth[j]], axis=0)
+        slope_copy(j).wait_recv()
+        up = jnp.concatenate([slope_own[j][...], slope_oth[j][...]], axis=0)
         grad = g0 if j < 2 else g1
         cols = pl.ds((j % 2) * 256, 256)
         for c in range(2):
@@ -568,7 +570,7 @@
         for c in range(2):
             for copy in rows_copies(m, c, values):
                 copy.wait_send()
-    rest = cot_copies() + h2_copies() + [slope_copy(), fin_copy(), x_copy(0), x_copy(1)]
+    rest = cot_copies() + h2_copies() + [fin_copy(), x_copy(0), x_copy(1)] + [slope_copy(j) for j in range(4)]
     rest += [w2_near(0), w2_near(1), w2_first()] + [w2_forward(d, k) for k, d in enumerate(far)]
     for h in range(2):
         rest += g1_copies(h) + g2_copies(h) + g3_copies(h)
@@ -598,13 +600,13 @@
         v((32, 8, 128), F32), v((32, 8, 128), F32), v((1024, 128), F32), v((1024, 128), BF),
         v((2, 256, 1024), BF), v((8, 256, 128), F32),
         *[v((32, 2, 128, 128), BF)] * 6, *[v((4, 4, 128, 128), BF)] * 6, v((2, 512, 1024), BF),
-        v((4, 512, 256), BF), v((2, 4, 256, 1024), BF), v((16, 1024), BF), *[v((4, 512, 256), BF)] * 2,
+        v((4, 512, 256), BF), v((2, 4, 256, 1024), BF), v((16, 1024), BF), *[v((512, 256), BF)] * 8,
         *[v((4, 4, 4, 16, 512), BF)] * 2, *[v((3, 4, 4, 16, 512), BF)] * 2,
         *[v((4, 4, 16, 512), F32)] * 2, *[v((3, 4, 16, 512), F32)] * 2, *[v((4, 16, 512), F32)] * 2,
         *[v((3, 16, 512), F32)] * 2, v((16, 1024), F32), v((8, 1024), F32),
         dma((11,)),
         *pair(32), *pair(4, 2), *pair(4, 4), *pair(4, 32), *pair(2, 2, 3), *pair(3), *pair(3),
-        *pair(16), *pair(3), *pair(2), *pair(1), *pair(3), *pair(2, 3), *pair(2, 3), *pair(2, 3), *pair(1),
+        *pair(16), *pair(3), *pair(2), *pair(4), *pair(3), *pair(2, 3), *pair(2, 3), *pair(2, 3), *pair(1),
     ]
     hidden2, grad_self, grad_neigh = pl.pallas_call(
         kernel,

time: 187 us -> 185 us (0.989)
  Pallas kernels: 182 us -> 180 us
    pallas_call x1, Pallas kernels: 182 us -> 180 us  [local_step(): pl.pallas_call(kernel, out_shape=(jax.ShapeDtypeStruct((2048, 256), BF),...]
where the time goes in v6:
time: 185 us
  Pallas kernels  180 us (97%)
  local copies, waits for them, and re-layouts  3.51 us (2%)
    pallas_call x1, Pallas kernels, local_step(): pl.pallas_call(kernel, out_shape=(jax.ShapeDtypeStruct((2048, 256), BF),...  180 us

profile of v6, /device:TPU:1, one launch (start us, length us, event | category | flops | bytes accessed | tf_op | source)
XLA Modules:
  0.0 184.9 jit_solution(13559837245949445866)
XLA Ops:
  0.6 1.3 pad_add_fusion.owners
  1.9 179.5 %sage.1 = (bf16[2048,256]{1,0:T(8,128)(2,1)}, f32[8,1024]{1,0:T(8,128)}, f32[8,1024]{1,0:T(8,128)}) custom-call(bf16[2048,512]{1,0:T(8,128)(2,1)} %feat_hbm.1, bf16[512,1024]{1,0:T(8,128)(2,1)} %ws1_hbm.1, bf16[512,1024]{1,0:T(8,128)(2,1)} %wn1_hbm.1, bf16[256,1024]{1,0:T(8,128)(2,1)} %ws2_hbm.1, bf16[256,1024]{1,0:T(8,128)(2,1)} %wn2_hbm.1, s32[32]{0:T(128)} %src1.1, ...), custom_call_target="tpu_custom_call" | custom-call | flops 10000000000 | bytes 16777216 | tf_op jit(solution)/shard_map/sage/pallas_call | solution.py:611
  181.4 0.0 copy-start.1
  181.4 0.0 copy-start
  181.4 2.3 %copy.20 = bf16[2048,256]{1,0:T(8,128)(2,1)} copy(bf16[2048,256]{1,0:T(8,128)(2,1)} %get-tuple-element.6) | data formatting | bytes 2097152
  183.7 0.0 copy-done.1
  183.7 0.6 copy.21
  184.3 0.0 copy-done
  184.3 0.6 copy.22
Async XLA Ops:
  181.4 2.3 %copy-start.1 = (f32[8,1024]{1,0:T(8,128)S(1)}, f32[8,1024]{1,0:T(8,128)}, u32[]{:S(2)}) copy-start(f32[8,1024]{1,0:T(8,128)} %get-tuple-element.7) | copy-start | bytes 98308
  181.4 2.9 %copy-start = (f32[8,1024]{1,0:T(8,128)S(1)}, f32[8,1024]{1,0:T(8,128)}, u32[]{:S(2)}) copy-start(f32[8,1024]{1,0:T(8,128)} %get-tuple-element.8) | copy-start | bytes 98308
